TPU v7x, 128 devices: a whole 4x4x4 slice. The times are simulated.
128 devices in a mesh: seq: 8 (over z, y_hi), grp: 16 (over y_lo, x, core).
Axes of the slice: x: 4, y: 4 (y_hi: 2, y_lo: 2; y = y_hi * 2 + y_lo), z: 4, core: 2. Of those that a mesh axis runs over, the one named last changes fastest.
Arguments:
- self_query: bfloat16 [16, 1024, 5120], P('grp', 'seq'), may hold values from -250 to 250
- self_key: bfloat16 [16, 1024, 5120], P('grp', 'seq'), may hold values from -12 to 12
- self_value: bfloat16 [16, 1024, 5120], P('grp', 'seq'), may hold values from -6 to 6
- self_upstream: bfloat16 [16, 1024, 5120], P('grp', 'seq'), may hold values from -6 to 6
- cross_query: bfloat16 [16, 1024, 5120], P('grp', 'seq'), may hold values from -250 to 250
- context_key: bfloat16 [512, 5120], replicated, may hold values from -12 to 12
- context_value: bfloat16 [512, 5120], replicated, may hold values from -6 to 6
- cross_upstream: bfloat16 [16, 1024, 5120], P('grp', 'seq'), may hold values from -6 to 6
Outputs:
- query_grad: bfloat16 [16, 1024, 5120], P('grp', 'seq')
- key_grad: bfloat16 [16, 1024, 5120], P('grp', 'seq')
- value_grad: bfloat16 [16, 1024, 5120], P('grp', 'seq')
- cross_query_grad: bfloat16 [16, 1024, 5120], P('grp', 'seq')
- context_key_grad: float32 [512, 5120], P(None, 'seq')
- context_value_grad: float32 [512, 5120], P(None, 'seq')
All inputs are finite; a program needn't handle non-finite values.
Results may differ from a plain program's by a relative error of at most 0.013.
Values may be sent and summed in bfloat16 or wider, within the bound.
A program may use at most 256 MiB of HBM per device.

v0:
```python
import jax
import jax.numpy as jnp
from jax import lax
from jax.sharding import PartitionSpec as P

HD = 128


def pick_rows(row_count, largest):
    block_rows = min(largest, row_count)
    while row_count % block_rows:
        block_rows = block_rows - 1
    return block_rows


def block_backward(queries, key_in, value_in, upstream):
    row_count, head_count, head_depth = queries.shape
    block_rows = pick_rows(row_count, 512)
    block_count = row_count // block_rows
    piece_rows = pick_rows(block_rows, 128)
    piece_count = block_rows // piece_rows
    scaling = HD ** (-0.5)

    def advance(totals, pieces):
        query_block, upstream_block = pieces
        scores = (
            jnp.einsum("nhe,mhe->hnm", query_block, key_in, preferred_element_type=jnp.float32)
            * scaling
        )
        weights = jax.nn.softmax(scores, axis=-1)
        rounded = weights.astype(jnp.bfloat16)
        output = jnp.einsum("hnm,mhe->nhe", rounded, value_in, preferred_element_type=jnp.float32)
        row_inner = jnp.sum(upstream_block.astype(jnp.float32) * output, axis=-1)
        grad_prob = jnp.einsum(
            "nhe,mhe->hnm", upstream_block, value_in, preferred_element_type=jnp.float32
        )
        grad_score = (
            weights * (grad_prob - jnp.transpose(row_inner)[:, :, None]) * scaling
        ).astype(jnp.bfloat16)
        query_grad = jnp.einsum(
            "hnm,mhe->nhe", grad_score, key_in, preferred_element_type=jnp.float32
        ).astype(jnp.bfloat16)
        score_split = grad_score.reshape(head_count, piece_count, piece_rows, grad_score.shape[2])
        weight_split = rounded.reshape(head_count, piece_count, piece_rows, rounded.shape[2])
        query_split = query_block.reshape(piece_count, piece_rows, head_count, head_depth)
        upstream_split = upstream_block.reshape(piece_count, piece_rows, head_count, head_depth)
        key_terms = jnp.einsum(
            "hgnm,gnhe->gmhe", score_split, query_split, preferred_element_type=jnp.float32
        )
        value_terms = jnp.einsum(
            "hgnm,gnhe->gmhe", weight_split, upstream_split, preferred_element_type=jnp.float32
        )
        key_sum = totals[0] + jnp.sum(key_terms, axis=0)
        value_sum = totals[1] + jnp.sum(value_terms, axis=0)
        return ((key_sum, value_sum), query_grad)

    zero_sum = jnp.zeros(key_in.shape, jnp.float32)
    blocked = (
        queries.reshape(block_count, block_rows, head_count, head_depth),
        upstream.reshape(block_count, block_rows, head_count, head_depth),
    )
    running, query_grads = lax.scan(advance, (zero_sum, zero_sum), blocked)
    return (query_grads.reshape(row_count, head_count, head_depth), running[0], running[1])


def shards(
    self_query,
    self_key,
    self_value,
    self_upstream,
    cross_query,
    context_key,
    context_value,
    cross_upstream,
):
    token_count = self_query.shape[1]
    full_width = self_query.shape[2]
    head_count = full_width // HD
    text_rows = context_key.shape[0]
    seq_count = lax.axis_size("seq")
    group_heads = head_count // seq_count

    def to_heads(tensor):
        return tensor.reshape(token_count, head_count, HD)

    def to_groups(tensor):
        return tensor.reshape(token_count, seq_count, group_heads, HD)

    pieces = (
        lax.all_to_all(to_groups(self_query[0]), "seq", split_axis=1, concat_axis=0, tiled=True),
        lax.all_to_all(to_groups(self_key[0]), "seq", split_axis=1, concat_axis=0, tiled=True),
        lax.all_to_all(to_groups(self_value[0]), "seq", split_axis=1, concat_axis=0, tiled=True),
        lax.all_to_all(to_groups(self_upstream[0]), "seq", split_axis=1, concat_axis=0, tiled=True),
    )
    rows = pieces[0].shape[0]
    items = pieces[0].shape[2]

    def flat(tensor):
        return tensor.reshape(rows, items, HD)

    query_part, key_part, value_part = block_backward(
        flat(pieces[0]), flat(pieces[1]), flat(pieces[2]), flat(pieces[3])
    )
    shape_back = (rows, 1, items, HD)
    query_grad, key_grad, value_grad = (
        lax.all_to_all(
            query_part.reshape(shape_back), "seq", split_axis=0, concat_axis=1, tiled=True
        ),
        lax.all_to_all(
            key_part.astype(jnp.bfloat16).reshape(shape_back),
            "seq",
            split_axis=0,
            concat_axis=1,
            tiled=True,
        ),
        lax.all_to_all(
            value_part.astype(jnp.bfloat16).reshape(shape_back),
            "seq",
            split_axis=0,
            concat_axis=1,
            tiled=True,
        ),
    )
    columns = full_width // seq_count
    offset = lax.axis_index("seq") * columns
    context_heads = context_key.reshape(text_rows, head_count, HD)
    value_heads = context_value.reshape(text_rows, head_count, HD)
    cross_grad, context_keys_part, context_values_part = block_backward(
        to_heads(cross_query[0]), context_heads, value_heads, to_heads(cross_upstream[0])
    )
    key_partial = context_keys_part.reshape(text_rows, full_width)
    value_partial = context_values_part.reshape(text_rows, full_width)
    key_whole, value_whole = lax.psum((key_partial, value_partial), ("seq", "grp"))
    key_total = lax.dynamic_slice_in_dim(key_whole, offset, columns, 1)
    value_total = lax.dynamic_slice_in_dim(value_whole, offset, columns, 1)
    shape_out = (1, token_count, full_width)
    return (
        query_grad.reshape(shape_out),
        key_grad.reshape(shape_out),
        value_grad.reshape(shape_out),
        cross_grad.reshape(shape_out),
        key_total,
        value_total,
    )


def solution(mesh):
    return jax.shard_map(
        shards,
        mesh=mesh,
        in_specs=(
            P("grp", "seq", None),
            P("grp", "seq", None),
            P("grp", "seq", None),
            P("grp", "seq", None),
            P("grp", "seq", None),
            P(),
            P(),
            P("grp", "seq", None),
        ),
        out_specs=(
            P("grp", "seq", None),
            P("grp", "seq", None),
            P("grp", "seq", None),
            P("grp", "seq", None),
            P(None, "seq"),
            P(None, "seq"),
        ),
        check_vma=False,
    )
```

profile of v0, /device:TPU:1, one launch (start us, length us, event | category | flops | bytes accessed | tf_op | source)
XLA Modules:
  0.0 414.7 jit_solution(14000686213218465211)
XLA Ops:
  9.7 8.5 %all-to-all-start = ((bf16[128,8,5,128]{0,3,2,1:T(8,128)(2,1)}), bf16[128,8,5,128]{0,3,2,1:T(8,128)(2,1)S(1)}, u32[]{:S(2)}, u32[]{:S(2)}) async-start(bf16[128,8,5,128]{0,3,2,1:T(8,128)(2,1)} %bitcast), calls=%async_computation | async-start | bytes 2621440 | tf_op jit(solution)/shard_map/all_to_all | solution.py:90
  21.4 7.9 %copy.145 = bf16[512,5120]{0,1:T(8,128)(2,1)} copy(bf16[512,5120]{1,0:T(8,128)(2,1)} %param.15) | data formatting | bytes 10485760 | tf_op jit(solution)/shard_map/reshape | solution.py:126
  29.3 10.0 %fusion.36 = (f32[40,128]{1,0:T(8,128)S(1)}, f32[40,128,512]{2,1,0:T(8,128)}) fusion(bf16[128,40,128]{0,2,1:T(8,128)(2,1)S(1)} %bitcast.198, bf16[512,40,128]{0,2,1:T(8,128)(2,1)} %bitcast.196), kind=kOutput, calls=%fused_computation.42 | convolution fusion | flops 678953472 | bytes 17059840 | tf_op jit(solution)/shard_map/while/body/eval_jaxpr/sub | solution.py:30
  39.3 6.6 %all-to-all-start.1 = ((bf16[128,8,5,128]{0,3,2,1:T(8,128)(2,1)}), bf16[128,8,5,128]{0,3,2,1:T(8,128)(2,1)}, u32[]{:S(2)}, u32[]{:S(2)}) async-start(bf16[128,8,5,128]{0,3,2,1:T(8,128)(2,1)} %bitcast.211), calls=%async_computation.1 | async-start | bytes 2621440 | tf_op jit(solution)/shard_map/all_to_all | solution.py:91
  46.0 7.3 %fusion.26 = bf16[40,128,512]{2,1,0:T(8,128)(2,1)} fusion(f32[40,128,512]{2,1,0:T(8,128)} %get-tuple-element.175, f32[40,128]{1,0:T(8,128)S(1)} %get-tuple-element.174), kind=kLoop, calls=%fused_computation.31 | loop fusion | flops 5242880 | bytes 15749120 | tf_op jit(solution)/shard_map/while/body/eval_jaxpr/convert_element_type | solution.py:31
  59.9 8.0 %copy.146 = bf16[512,5120]{0,1:T(8,128)(2,1)} copy(bf16[512,5120]{1,0:T(8,128)(2,1)} %param.16) | data formatting | bytes 10485760 | tf_op jit(solution)/shard_map/reshape | solution.py:127
  73.4 6.7 %all-to-all-start.2 = ((bf16[128,8,5,128]{0,3,2,1:T(8,128)(2,1)}), bf16[128,8,5,128]{0,3,2,1:T(8,128)(2,1)}, u32[]{:S(2)}, u32[]{:S(2)}) async-start(bf16[128,8,5,128]{0,3,2,1:T(8,128)(2,1)} %bitcast.212), calls=%async_computation.2 | async-start | bytes 2621440 | tf_op jit(solution)/shard_map/all_to_all | solution.py:93
  80.1 8.3 %multiply_convert_fusion.1 = bf16[40,128,512]{2,1,0:T(8,128)(2,1)} fusion(f32[40,128]{1,0:T(8,128)S(1)} %bitcast.223, f32[40,128,512]{2,1,0:T(8,128)} %get-tuple-element.175, f32[40,128]{1,0:T(8,128)S(1)} %get-tuple-element.174, bf16[128,40,128]{0,2,1:T(8,128)(2,1)S(1)} %bitcast.203, bf16[512,40,128]{0,2,1:T(8,128)(2,1)} %bitcast.208), kind=kOutput, calls=%fused_computation.25 | convolution fusion | flops 684195840 | bytes 22323200 | tf_op jit(solution)/shard_map/while/body/eval_jaxpr/nhe,mhe->hnm/dot_general | solution.py:34
  88.4 9.4 %all-to-all-done.2 = bf16[128,8,5,128]{0,3,2,1:T(8,128)(2,1)} async-done(((bf16[128,8,5,128]{0,3,2,1:T(8,128)(2,1)}), bf16[128,8,5,128]{0,3,2,1:T(8,128)(2,1)}, u32[]{:S(2)}, u32[]{:S(2)}) %all-to-all-start.2) | async-done | bytes 1310752 | tf_op jit(solution)/shard_map/all_to_all | solution.py:93
  102.6 7.8 %fusion.37 = f32[40,512,128]{1,2,0:T(8,128)} fusion(bf16[128,40,128]{0,2,1:T(8,128)(2,1)S(1)} %bitcast.199, bf16[40,128,512]{2,1,0:T(8,128)(2,1)} %multiply_convert_fusion.1), kind=kOutput, calls=%fused_computation.43 | convolution fusion | flops 671088640 | bytes 17039360 | tf_op jit(solution)/shard_map/while/body/eval_jaxpr/hgnm,gnhe->gmhe/dot_general | solution.py:47
  110.4 11.5 %copy.127 = f32[512,5120]{1,0:T(8,128)} copy(f32[512,5120]{0,1:T(8,128)} %bitcast.193) | data formatting | bytes 20971520 | tf_op jit(solution)/shard_map/reshape | solution.py:131
  121.9 8.0 %fusion.38 = f32[40,512,128]{1,2,0:T(8,128)} fusion(bf16[128,40,128]{0,2,1:T(8,128)(2,1)S(1)} %bitcast.204, bf16[40,128,512]{2,1,0:T(8,128)(2,1)} %fusion.26), kind=kOutput, calls=%fused_computation.44 | convolution fusion | flops 671088640 | bytes 17039360 | tf_op jit(solution)/shard_map/while/body/eval_jaxpr/hgnm,gnhe->gmhe/dot_general | solution.py:50
  129.8 11.5 %copy.128 = f32[512,5120]{1,0:T(8,128)} copy(f32[512,5120]{0,1:T(8,128)} %bitcast.192) | data formatting | bytes 20971520 | tf_op jit(solution)/shard_map/reshape | solution.py:132
  152.1 76.3 %while.3 = (s32[]{:T(128)}, f32[1024,5,128]{0,2,1:T(8,128)}, f32[1024,5,128]{0,2,1:T(8,128)}, bf16[2,512,5,128]{3,1,0,2:T(8,128)(2,1)}, bf16[2,512,5,128]{3,1,0,...) while((s32[]{:T(128)}, f32[1024,5,128]{0,2,1:T(8,128)}, ...), condition=%wide.region_4.0_spmd.clone, body=%wide.region_0.4_spmd.clone.sunk | while | flops 4056676864 | bytes 158648704 | solution.py:62
  153.5 8.6 %fusion.92 = (f32[5,512]{1,0:T(8,128)S(1)}, f32[5,512,1024]{2,1,0:T(8,128)}) fusion(bf16[1024,5,128]{2,0,1:T(8,128)(2,1)} %get-tuple-element.260, bf16[1,512,5,128]{3,1,0,2:T(8,128)(2,1)S(1)} %get-tuple-element.231), kind=kOutput, calls=%fused_computation.41.clone.1 | convolution fusion | flops 678953984 | bytes 12462080 | tf_op jit(solution)/shard_map/while/body/eval_jaxpr/sub | solution.py:30
  170.3 7.0 %multiply_convert_fusion.3 = bf16[5,512,1024]{2,1,0:T(8,128)(2,1)} fusion(f32[5,512]{1,0:T(8,128)S(1)} %bitcast.224, f32[5,512,1024]{2,1,0:T(8,128)} %get-tuple-element.232, f32[5,512]{1,0:T(8,128)S(1)} %get-tuple-element.233, bf16[1024,5,128]{0,2,1:T(8,128)(2,1)S(1)} %copy-done.7, bf16[1,512,5,128]{3,1,0,2:T(8,128)(2,1)S(1)} %get-tuple-element.234), kind=kOutput, calls=%fused_computation.1.clone.1 | convolution fusion | flops 684195840 | bytes 17715200 | tf_op jit(solution)/shard_map/while/body/eval_jaxpr/nhe,mhe->hnm/dot_general | solution.py:34
  190.7 8.5 %fusion.92 = (f32[5,512]{1,0:T(8,128)S(1)}, f32[5,512,1024]{2,1,0:T(8,128)}) fusion(bf16[1024,5,128]{2,0,1:T(8,128)(2,1)} %get-tuple-element.260, bf16[1,512,5,128]{3,1,0,2:T(8,128)(2,1)S(1)} %get-tuple-element.231), kind=kOutput, calls=%fused_computation.41.clone.1 | convolution fusion | flops 678953984 | bytes 12462080 | tf_op jit(solution)/shard_map/while/body/eval_jaxpr/sub | solution.py:30
  207.4 7.2 %multiply_convert_fusion.3 = bf16[5,512,1024]{2,1,0:T(8,128)(2,1)} fusion(f32[5,512]{1,0:T(8,128)S(1)} %bitcast.224, f32[5,512,1024]{2,1,0:T(8,128)} %get-tuple-element.232, f32[5,512]{1,0:T(8,128)S(1)} %get-tuple-element.233, bf16[1024,5,128]{0,2,1:T(8,128)(2,1)S(1)} %copy-done.7, bf16[1,512,5,128]{3,1,0,2:T(8,128)(2,1)S(1)} %get-tuple-element.234), kind=kOutput, calls=%fused_computation.1.clone.1 | convolution fusion | flops 684195840 | bytes 17715200 | tf_op jit(solution)/shard_map/while/body/eval_jaxpr/nhe,mhe->hnm/dot_general | solution.py:34
  214.6 6.2 %bitcast_add_fusion.4 = f32[1024,5,128]{0,2,1:T(8,128)} fusion(f32[1024,5,128]{0,2,1:T(8,128)} %get-tuple-element.246, bf16[4,128,5,128]{3,1,0,2:T(8,128)(2,1)S(1)} %bitcast.195, bf16[5,4,128,1024]{3,2,1,0:T(8,128)(2,1)} %bitcast.189, pred[]{:T(512)S(6)} %compare.3), kind=kOutput, calls=%fused_computation.9.clone.1 | convolution fusion | flops 672399360 | bytes 11141121 | tf_op jit(solution)/shard_map/while/body/eval_jaxpr/hgnm,gnhe->gmhe/dot_general | solution.py:47
  232.0 6.9 %all-to-all-start.4 = ((bf16[1024,1,5,128]{3,2,1,0:T(8,128)(2,1)}), bf16[1024,1,5,128]{3,2,1,0:T(8,128)(2,1)}, u32[]{:S(2)}, u32[]{:S(2)}) async-start(bf16[1024,1,5,128]{3,2,1,0:T(8,128)(2,1)} %copy.110), calls=%async_computation.4 | async-start | bytes 4194304 | tf_op jit(solution)/shard_map/all_to_all | solution.py:106
  242.0 23.9 %all-to-all-done.4 = bf16[1024,1,5,128]{3,2,1,0:T(8,128)(2,1)} async-done(((bf16[1024,1,5,128]{3,2,1,0:T(8,128)(2,1)}), bf16[1024,1,5,128]{3,2,1,0:T(8,128)(2,1)}, u32[]{:S(2)}, u32[]{:S(2)}) %all-to-all-start.4) | async-done | bytes 1310752 | tf_op jit(solution)/shard_map/all_to_all | solution.py:106
  274.5 24.0 %all-to-all-done.5 = bf16[1024,1,5,128]{3,2,1,0:T(8,128)(2,1)} async-done(((bf16[1024,1,5,128]{3,2,1,0:T(8,128)(2,1)}), bf16[1024,1,5,128]{3,2,1,0:T(8,128)(2,1)}, u32[]{:S(2)}, u32[]{:S(2)}) %all-to-all-start.5) | async-done | bytes 1310752 | tf_op jit(solution)/shard_map/all_to_all | solution.py:109
  322.5 14.6 %all-to-all-done.6 = bf16[1024,1,5,128]{3,2,1,0:T(8,128)(2,1)S(1)} async-done(((bf16[1024,1,5,128]{3,2,1,0:T(8,128)(2,1)}), bf16[1024,1,5,128]{3,2,1,0:T(8,128)(2,1)S(1)}, u32[]{:S(2)}, u32[]{:S(2)}) %all-to-all-start.6) | async-done | bytes 1310752 | tf_op jit(solution)/shard_map/all_to_all | solution.py:116
  339.5 65.0 %all-reduce.3.cloned.1.call-done = (f32[512,5120]{1,0:T(8,128)}, f32[512,5120]{1,0:T(8,128)}) async-done(((f32[512,5120]{1,0:T(8,128)}, f32[512,5120]{1,0:T(8,128)}), (f32[512,5120]{1,0:T(8,128)}, f32[512,5120]{1,0:T(8,128)})) %all-reduce.3.cloned.1.call-update) | async-done | bytes 20971536 | tf_op jit(solution)/shard_map/psum | solution.py:133
  (99 shorter events, 117.1 us)
Async XLA Ops:
  7.2 11.0 %copy-start.5 = (bf16[1,128,5120]{2,1,0:T(8,128)(2,1)S(1)}, bf16[1,128,5120]{2,1,0:T(8,128)(2,1)}, u32[]{:S(2)}) copy-start(bf16[1,128,5120]{2,1,0:T(8,128)(2,1)} %param.11) | copy-start | bytes 3932164
  9.7 29.6 %all-to-all-start = ((bf16[128,8,5,128]{0,3,2,1:T(8,128)(2,1)}), bf16[128,8,5,128]{0,3,2,1:T(8,128)(2,1)S(1)}, u32[]{:S(2)}, u32[]{:S(2)}) async-start(bf16[128,8,5,128]{0,3,2,1:T(8,128)(2,1)} %bitcast), calls=%async_computation | async-start | bytes 2621440 | tf_op jit(solution)/shard_map/all_to_all | solution.py:90
  39.3 13.9 %copy-start.3 = (bf16[128,8,5,128]{0,3,2,1:T(8,128)(2,1)}, bf16[128,8,5,128]{0,3,2,1:T(8,128)(2,1)S(1)}, u32[]{:S(2)}) copy-start(bf16[128,8,5,128]{0,3,2,1:T(8,128)(2,1)S(1)} %all-to-all-done) | copy-start | bytes 3932164
  39.3 34.1 %all-to-all-start.1 = ((bf16[128,8,5,128]{0,3,2,1:T(8,128)(2,1)}), bf16[128,8,5,128]{0,3,2,1:T(8,128)(2,1)}, u32[]{:S(2)}, u32[]{:S(2)}) async-start(bf16[128,8,5,128]{0,3,2,1:T(8,128)(2,1)} %bitcast.211), calls=%async_computation.1 | async-start | bytes 2621440 | tf_op jit(solution)/shard_map/all_to_all | solution.py:91
  73.4 24.4 %all-to-all-start.2 = ((bf16[128,8,5,128]{0,3,2,1:T(8,128)(2,1)}), bf16[128,8,5,128]{0,3,2,1:T(8,128)(2,1)}, u32[]{:S(2)}, u32[]{:S(2)}) async-start(bf16[128,8,5,128]{0,3,2,1:T(8,128)(2,1)} %bitcast.212), calls=%async_computation.2 | async-start | bytes 2621440 | tf_op jit(solution)/shard_map/all_to_all | solution.py:93
  97.9 51.0 %all-to-all-start.3 = ((bf16[128,8,5,128]{0,3,2,1:T(8,128)(2,1)}), bf16[128,8,5,128]{0,3,2,1:T(8,128)(2,1)}, u32[]{:S(2)}, u32[]{:S(2)}) async-start(bf16[128,8,5,128]{0,3,2,1:T(8,128)(2,1)} %bitcast.210), calls=%async_computation.3 | async-start | bytes 2621440 | tf_op jit(solution)/shard_map/all_to_all | solution.py:92
  102.4 302.1 %all-reduce.3.cloned.1.call-start = ((), (), s32[]{:S(2)}) async-start(), calls=%async_computation.7 | async-start | bytes 41943040 | tf_op jit(solution)/shard_map/psum | solution.py:133
  162.1 5.8 %copy-start.7 = (bf16[1024,5,128]{0,2,1:T(8,128)(2,1)S(1)}, bf16[1024,5,128]{0,2,1:T(8,128)(2,1)}, u32[]{:S(2)}) copy-start(bf16[1024,5,128]{0,2,1:T(8,128)(2,1)} %get-tuple-element.262) | copy-start | bytes 3932164 | tf_op jit(solution)/shard_map/while
  177.3 5.3 %slice-start = ((s8[5242880]{0:T(1024)(128)(4,1)}), s8[1048576]{0:T(1024)(128)(4,1)S(1)}, s32[]{:S(2)}) async-start(s8[5242880]{0:T(1024)(128)(4,1)} %bitcast.186), calls=%async_computation.8 | async-start | bytes 2097152 | tf_op jit(solution)/shard_map/while
  177.3 5.3 %slice-start.1 = ((s8[5242880]{0:T(1024)(128)(4,1)}), s8[4194304]{0:T(1024)(128)(4,1)S(1)}, s32[]{:S(2)}) async-start(s8[5242880]{0:T(1024)(128)(4,1)} %bitcast.186), calls=%async_computation.9 | async-start | bytes 8388608 | tf_op jit(solution)/shard_map/while
  177.3 7.9 %slice-start.2 = ((s8[5242880]{0:T(1024)(128)(4,1)}), s8[4194304]{0:T(1024)(128)(4,1)S(1)}, s32[]{:S(2)}) async-start(s8[5242880]{0:T(1024)(128)(4,1)} %bitcast.190), calls=%async_computation.10 | async-start | bytes 8388608 | tf_op jit(solution)/shard_map/while
  182.7 3.8 copy-start.8
  199.2 5.8 %copy-start.7 = (bf16[1024,5,128]{0,2,1:T(8,128)(2,1)S(1)}, bf16[1024,5,128]{0,2,1:T(8,128)(2,1)}, u32[]{:S(2)}) copy-start(bf16[1024,5,128]{0,2,1:T(8,128)(2,1)} %get-tuple-element.262) | copy-start | bytes 3932164 | tf_op jit(solution)/shard_map/while
  214.6 6.2 %slice-start = ((s8[5242880]{0:T(1024)(128)(4,1)}), s8[1048576]{0:T(1024)(128)(4,1)S(1)}, s32[]{:S(2)}) async-start(s8[5242880]{0:T(1024)(128)(4,1)} %bitcast.186), calls=%async_computation.8 | async-start | bytes 2097152 | tf_op jit(solution)/shard_map/while
  214.6 6.2 %slice-start.1 = ((s8[5242880]{0:T(1024)(128)(4,1)}), s8[4194304]{0:T(1024)(128)(4,1)S(1)}, s32[]{:S(2)}) async-start(s8[5242880]{0:T(1024)(128)(4,1)} %bitcast.186), calls=%async_computation.9 | async-start | bytes 8388608 | tf_op jit(solution)/shard_map/while
  214.6 11.0 %slice-start.2 = ((s8[5242880]{0:T(1024)(128)(4,1)}), s8[4194304]{0:T(1024)(128)(4,1)S(1)}, s32[]{:S(2)}) async-start(s8[5242880]{0:T(1024)(128)(4,1)} %bitcast.190), calls=%async_computation.10 | async-start | bytes 8388608 | tf_op jit(solution)/shard_map/while
  220.7 4.8 %slice-start.3 = ((s8[5242880]{0:T(1024)(128)(4,1)}), s8[1048576]{0:T(1024)(128)(4,1)S(1)}, s32[]{:S(2)}) async-start(s8[5242880]{0:T(1024)(128)(4,1)} %bitcast.190), calls=%async_computation.11 | async-start | bytes 2097152 | tf_op jit(solution)/shard_map/while
  220.8 4.8 %copy-start.6 = (bf16[1024,5,128]{2,0,1:T(8,128)(2,1)S(1)}, bf16[1024,5,128]{2,0,1:T(8,128)(2,1)}, u32[]{:S(2)}) copy-start(bf16[1024,5,128]{2,0,1:T(8,128)(2,1)} %get-tuple-element.260) | copy-start | bytes 3932164 | tf_op jit(solution)/shard_map/while
  220.8 4.8 %copy-start.8 = (bf16[2,512,5,128]{3,1,0,2:T(8,128)(2,1)S(1)}, bf16[2,512,5,128]{3,1,0,2:T(8,128)(2,1)}, u32[]{:S(2)}) copy-start(bf16[2,512,5,128]{3,1,0,2:T(8,128)(2,1)} %get-tuple-element.248) | copy-start | bytes 3932164 | tf_op jit(solution)/shard_map/while
  232.0 6.9 %copy-start.1 = (f32[1024,5,128]{0,2,1:T(8,128)S(1)}, f32[1024,5,128]{0,2,1:T(8,128)}, u32[]{:S(2)}) copy-start(f32[1024,5,128]{0,2,1:T(8,128)} %get-tuple-element.75) | copy-start | bytes 7864324
  232.0 33.9 %all-to-all-start.4 = ((bf16[1024,1,5,128]{3,2,1,0:T(8,128)(2,1)}), bf16[1024,1,5,128]{3,2,1,0:T(8,128)(2,1)}, u32[]{:S(2)}, u32[]{:S(2)}) async-start(bf16[1024,1,5,128]{3,2,1,0:T(8,128)(2,1)} %copy.110), calls=%async_computation.4 | async-start | bytes 4194304 | tf_op jit(solution)/shard_map/all_to_all | solution.py:106
  242.0 29.4 %copy-start.2 = (f32[1024,5,128]{0,2,1:T(8,128)S(1)}, f32[1024,5,128]{0,2,1:T(8,128)}, u32[]{:S(2)}) copy-start(f32[1024,5,128]{0,2,1:T(8,128)} %get-tuple-element.76) | copy-start | bytes 7864324
  265.9 32.7 %all-to-all-start.5 = ((bf16[1024,1,5,128]{3,2,1,0:T(8,128)(2,1)}), bf16[1024,1,5,128]{3,2,1,0:T(8,128)(2,1)}, u32[]{:S(2)}, u32[]{:S(2)}) async-start(bf16[1024,1,5,128]{3,2,1,0:T(8,128)(2,1)} %bitcast.206), calls=%async_computation.5 | async-start | bytes 4194304 | tf_op jit(solution)/shard_map/all_to_all | solution.py:109
  298.5 38.5 %all-to-all-start.6 = ((bf16[1024,1,5,128]{3,2,1,0:T(8,128)(2,1)}), bf16[1024,1,5,128]{3,2,1,0:T(8,128)(2,1)S(1)}, u32[]{:S(2)}, u32[]{:S(2)}) async-start(bf16[1024,1,5,128]{3,2,1,0:T(8,128)(2,1)} %bitcast.205), calls=%async_computation.6 | async-start | bytes 4194304 | tf_op jit(solution)/shard_map/all_to_all | solution.py:116
  (7 other events, 13.3 us)
Sparse Core Ops, SparseCore 0:
  141.5 262.9 all-reduce.2
where the time goes:
time: 416 us; the launch traced here: 415 us
  waiting for transfers between devices  137 us (33%)
  matrix products  102 us (25%)
  local copies, waits for them, and re-layouts  97.9 us (24%)
  starting transfers between devices  44.4 us (11%)
  other arithmetic  18.9 us (5%)
  between operations  14.2 us (3%)
    psum x1, waiting for transfers between devices, shards(): lax.psum((key_partial, value_partial), ('seq', 'grp'))  65 us
    sub x3, matrix products, advance(): weights = jax.nn.softmax(scores, axis=-1)  27.1 us
    all_to_all x1, waiting for transfers between devices, shards(): lax.all_to_all(key_part.astype(jnp.bfloat16).reshape(shape_back), 'seq',...  24 us
    all_to_all x1, waiting for transfers between devices, shards(): lax.all_to_all(query_part.reshape(shape_back), 'seq', split_axis=0, conca...  23.9 us
    dot_general x3, matrix products, advance(): jnp.einsum('nhe,mhe->hnm', upstream_block, value_in, preferred_element_ty...  22.5 us
    unnamed x20, local copies, waits for them, and re-layouts  21 us
    dot_general x3, matrix products, advance(): jnp.einsum('hgnm,gnhe->gmhe', score_split, query_split, preferred_element...  19.3 us
    convert_element_type x3, other arithmetic, advance(): rounded = weights.astype(jnp.bfloat16)  18.9 us
  transfers between devices with their start and end apart: 8, of which 5 were waited for; matrix products, arithmetic and copies ran while one was open for 50% of the time, Pallas kernels for 0%

commit v1 on v0

--- a/solution.py
+++ b/solution.py
@@ -130,7 +130,7 @@
     )
     key_partial = context_keys_part.reshape(text_rows, full_width)
     value_partial = context_values_part.reshape(text_rows, full_width)
-    key_whole, value_whole = lax.psum((key_partial, value_partial), ("seq", "grp"))
+    key_whole, value_whole = lax.psum(lax.psum((key_partial, value_partial), "grp"), "seq")
     key_total = lax.dynamic_slice_in_dim(key_whole, offset, columns, 1)
     value_total = lax.dynamic_slice_in_dim(value_whole, offset, columns, 1)
     shape_out = (1, token_count, full_width)

time: 416 us -> 1280 us (3.08)
  waiting for transfers between devices: 137 us -> 1030 us
    psum x1 -> x2, waiting for transfers between devices: 65 us -> 794 us  [the longest x1 554 us: shards(): lax.psum(lax.psum((key_partial, value_partial), 'grp'), 'seq')]
    all_to_all x1, waiting for transfers between devices: 0.01 us -> 29.7 us  [shards(): lax.all_to_all(to_groups(self_key[0]), 'seq', split_axis=1, concat_axis=0...]
    all_to_all x1, waiting for transfers between devices: 0.01 us -> 27.9 us  [shards(): lax.all_to_all(to_groups(self_query[0]), 'seq', split_axis=1, concat_axis...]
    all_to_all x1, waiting for transfers between devices: 0.01 us -> 26.6 us  [shards(): lax.all_to_all(to_groups(self_value[0]), 'seq', split_axis=1, concat_axis...]
    all_to_all x1, waiting for transfers between devices: 23.9 us -> 45.1 us  [shards(): lax.all_to_all(query_part.reshape(shape_back), 'seq', split_axis=0, conca...]
    all_to_all x1, waiting for transfers between devices: 24 us -> 44.7 us  [shards(): lax.all_to_all(key_part.astype(jnp.bfloat16).reshape(shape_back), 'seq',...]
    all_to_all x1, waiting for transfers between devices: 9.43 us -> 29.6 us  [shards(): lax.all_to_all(to_groups(self_upstream[0]), 'seq', split_axis=1, concat_a...]
    all_to_all x1, waiting for transfers between devices: 14.6 us -> 29.4 us  [shards(): lax.all_to_all(value_part.astype(jnp.bfloat16).reshape(shape_back), 'seq'...]
  transfers between devices with their start and end apart: 8 -> 9, of which waited for: 5 -> 9; matrix products, arithmetic and copies ran while one was open for 50% -> 9% of each run, Pallas kernels for 0% -> 0%
where the time goes in v1:
time: 1280 us; the launch traced here: 1270 us
  waiting for transfers between devices  1030 us (80%)
  local copies, waits for them, and re-layouts  94.6 us (7%)
  matrix products  90.5 us (7%)
  starting transfers between devices  31.6 us (2%)
  other arithmetic  16.4 us (1%)
  between operations  14.3 us (1%)
    psum x1, waiting for transfers between devices, shards(): lax.psum(lax.psum((key_partial, value_partial), 'grp'), 'seq')  554 us
    psum x1, waiting for transfers between devices, shards(): lax.psum((key_partial, value_partial), 'grp')  240 us
    all_to_all x1, waiting for transfers between devices, shards(): lax.all_to_all(query_part.reshape(shape_back), 'seq', split_axis=0, conca...  45.1 us
    all_to_all x1, waiting for transfers between devices, shards(): lax.all_to_all(key_part.astype(jnp.bfloat16).reshape(shape_back), 'seq',...  44.7 us
    all_to_all x1, waiting for transfers between devices, shards(): lax.all_to_all(to_groups(self_key[0]), 'seq', split_axis=1, concat_axis=0...  29.7 us
    all_to_all x1, waiting for transfers between devices, shards(): lax.all_to_all(to_groups(self_upstream[0]), 'seq', split_axis=1, concat_a...  29.6 us
    all_to_all x1, waiting for transfers between devices, shards(): lax.all_to_all(value_part.astype(jnp.bfloat16).reshape(shape_back), 'seq'...  29.4 us
    all_to_all x1, waiting for transfers between devices, shards(): lax.all_to_all(to_groups(self_query[0]), 'seq', split_axis=1, concat_axis...  27.9 us
  transfers between devices with their start and end apart: 9, of which 9 were waited for; matrix products, arithmetic and copies ran while one was open for 9% of the time, Pallas kernels for 0%

profile of v1, /device:TPU:1, one launch (start us, length us, event | category | flops | bytes accessed | tf_op | source)
XLA Modules:
  0.0 1274.7 jit_solution(9623007065652247539)
XLA Ops:
  10.8 7.9 copy.145
  18.7 7.9 copy.146
  26.6 9.8 fusion.36
  36.5 5.7 fusion.26
  42.1 5.5 fusion.38
  62.3 11.5 copy.127
  73.8 11.5 copy.128
  85.5 240.2 %all-reduce.5.cloned.1.call-done = (f32[512,5120]{1,0:T(8,128)}, f32[512,5120]{1,0:T(8,128)}) async-done(((f32[512,5120]{1,0:T(8,128)}, f32[512,5120]{1,0:T(8,128)}), (f32[512,5120]{1,0:T(8,128)}, f32[512,5120]{1,0:T(8,128)})) %all-reduce.5.cloned.1.call-update) | async-done | bytes 20971536 | tf_op jit(solution)/shard_map/psum | solution.py:133
  328.4 6.6 all-to-all-start
  336.4 27.9 %all-to-all-done = bf16[128,8,5,128]{0,3,2,1:T(8,128)(2,1)S(1)} async-done(((bf16[128,8,5,128]{0,3,2,1:T(8,128)(2,1)}), bf16[128,8,5,128]{0,3,2,1:T(8,128)(2,1)S(1)}, u32[]{:S(2)}, u32[]{:S(2)}) %all-to-all-start) | async-done | bytes 1310752 | tf_op jit(solution)/shard_map/all_to_all | solution.py:90
  370.3 29.7 %all-to-all-done.1 = bf16[128,8,5,128]{0,3,2,1:T(8,128)(2,1)S(1)} async-done(((bf16[128,8,5,128]{0,3,2,1:T(8,128)(2,1)}), bf16[128,8,5,128]{0,3,2,1:T(8,128)(2,1)S(1)}, u32[]{:S(2)}, u32[]{:S(2)}) %all-to-all-start.1) | async-done | bytes 1310752 | tf_op jit(solution)/shard_map/all_to_all | solution.py:91
  406.8 29.6 %all-to-all-done.2 = bf16[128,8,5,128]{0,3,2,1:T(8,128)(2,1)} async-done(((bf16[128,8,5,128]{0,3,2,1:T(8,128)(2,1)}), bf16[128,8,5,128]{0,3,2,1:T(8,128)(2,1)}, u32[]{:S(2)}, u32[]{:S(2)}) %all-to-all-start.2) | async-done | bytes 1310752 | tf_op jit(solution)/shard_map/all_to_all | solution.py:93
  446.0 26.6 %all-to-all-done.3 = bf16[128,8,5,128]{0,3,2,1:T(8,128)(2,1)} async-done(((bf16[128,8,5,128]{0,3,2,1:T(8,128)(2,1)}), bf16[128,8,5,128]{0,3,2,1:T(8,128)(2,1)}, u32[]{:S(2)}, u32[]{:S(2)}) %all-to-all-start.3) | async-done | bytes 1310752 | tf_op jit(solution)/shard_map/all_to_all | solution.py:92
  475.8 72.3 %while.3 = (s32[]{:T(128)}, f32[1024,5,128]{0,2,1:T(8,128)}, f32[1024,5,128]{0,2,1:T(8,128)}, bf16[2,512,5,128]{3,1,0,2:T(8,128)(2,1)}, bf16[2,512,5,128]{3,1,0,...) while((s32[]{:T(128)}, f32[1024,5,128]{0,2,1:T(8,128)}, ...), condition=%wide.region_4.0_spmd.clone, body=%wide.region_0.4_spmd.clone.sunk | while | flops 4056676864 | bytes 158648704 | solution.py:62
  477.2 8.4 fusion.92
  493.4 6.7 multiply_convert_fusion.3
  512.1 8.5 fusion.92
  528.3 6.7 multiply_convert_fusion.3
  534.9 6.0 bitcast_add_fusion.4
  559.5 45.1 %all-to-all-done.4 = bf16[1024,1,5,128]{3,2,1,0:T(8,128)(2,1)} async-done(((bf16[1024,1,5,128]{3,2,1,0:T(8,128)(2,1)}), bf16[1024,1,5,128]{3,2,1,0:T(8,128)(2,1)}, u32[]{:S(2)}, u32[]{:S(2)}) %all-to-all-start.4) | async-done | bytes 1310752 | tf_op jit(solution)/shard_map/all_to_all | solution.py:106
  612.1 44.7 %all-to-all-done.5 = bf16[1024,1,5,128]{3,2,1,0:T(8,128)(2,1)} async-done(((bf16[1024,1,5,128]{3,2,1,0:T(8,128)(2,1)}), bf16[1024,1,5,128]{3,2,1,0:T(8,128)(2,1)}, u32[]{:S(2)}, u32[]{:S(2)}) %all-to-all-start.5) | async-done | bytes 1310752 | tf_op jit(solution)/shard_map/all_to_all | solution.py:109
  660.4 5.6 convolution_convert_fusion.1
  678.7 29.4 %all-to-all-done.6 = bf16[1024,1,5,128]{3,2,1,0:T(8,128)(2,1)S(1)} async-done(((bf16[1024,1,5,128]{3,2,1,0:T(8,128)(2,1)}), bf16[1024,1,5,128]{3,2,1,0:T(8,128)(2,1)S(1)}, u32[]{:S(2)}, u32[]{:S(2)}) %all-to-all-start.6) | async-done | bytes 1310752 | tf_op jit(solution)/shard_map/all_to_all | solution.py:116
  710.5 554.0 %all-reduce.7.cloned.1.call-done = (f32[512,5120]{1,0:T(8,128)}, f32[512,5120]{1,0:T(8,128)}) async-done(((f32[512,5120]{1,0:T(8,128)}, f32[512,5120]{1,0:T(8,128)}), (f32[512,5120]{1,0:T(8,128)}, f32[512,5120]{1,0:T(8,128)})) %all-reduce.7.cloned.1.call-update) | async-done | bytes 20971536 | tf_op jit(solution)/shard_map/psum | solution.py:133
  (109 shorter events, 124.9 us)
Async XLA Ops:
  7.2 318.5 %all-reduce.5.cloned.1.call-start = ((), (), s32[]{:S(2)}) async-start(), calls=%async_computation.7 | async-start | bytes 41943040 | tf_op jit(solution)/shard_map/psum | solution.py:133
  36.5 15.5 %slice-start.4 = ((s8[10485760]{0:T(1024)(128)(4,1)}), s8[4194304]{0:T(1024)(128)(4,1)S(1)}, s32[]{:S(2)}) async-start(s8[10485760]{0:T(1024)(128)(4,1)} %bitcast.198), calls=%async_computation.13 | async-start | bytes 8388608
  42.1 9.8 slice-start.5
  42.1 9.8 slice-start.6
  56.8 5.5 copy-start.3
  85.3 1179.3 %all-reduce.7.cloned.1.call-start = ((), (), s32[]{:S(2)}) async-start(), calls=%async_computation.8 | async-start | bytes 41943040 | tf_op jit(solution)/shard_map/psum | solution.py:133
  327.0 8.0 copy-start.5
  328.4 35.9 %all-to-all-start = ((bf16[128,8,5,128]{0,3,2,1:T(8,128)(2,1)}), bf16[128,8,5,128]{0,3,2,1:T(8,128)(2,1)S(1)}, u32[]{:S(2)}, u32[]{:S(2)}) async-start(bf16[128,8,5,128]{0,3,2,1:T(8,128)(2,1)} %bitcast), calls=%async_computation | async-start | bytes 2621440 | tf_op jit(solution)/shard_map/all_to_all | solution.py:90
  364.3 35.7 %all-to-all-start.1 = ((bf16[128,8,5,128]{0,3,2,1:T(8,128)(2,1)}), bf16[128,8,5,128]{0,3,2,1:T(8,128)(2,1)S(1)}, u32[]{:S(2)}, u32[]{:S(2)}) async-start(bf16[128,8,5,128]{0,3,2,1:T(8,128)(2,1)} %bitcast.214), calls=%async_computation.1 | async-start | bytes 2621440 | tf_op jit(solution)/shard_map/all_to_all | solution.py:91
  400.1 36.3 %all-to-all-start.2 = ((bf16[128,8,5,128]{0,3,2,1:T(8,128)(2,1)}), bf16[128,8,5,128]{0,3,2,1:T(8,128)(2,1)}, u32[]{:S(2)}, u32[]{:S(2)}) async-start(bf16[128,8,5,128]{0,3,2,1:T(8,128)(2,1)} %bitcast.215), calls=%async_computation.2 | async-start | bytes 2621440 | tf_op jit(solution)/shard_map/all_to_all | solution.py:93
  436.4 36.2 %all-to-all-start.3 = ((bf16[128,8,5,128]{0,3,2,1:T(8,128)(2,1)}), bf16[128,8,5,128]{0,3,2,1:T(8,128)(2,1)}, u32[]{:S(2)}, u32[]{:S(2)}) async-start(bf16[128,8,5,128]{0,3,2,1:T(8,128)(2,1)} %bitcast.213), calls=%async_computation.3 | async-start | bytes 2621440 | tf_op jit(solution)/shard_map/all_to_all | solution.py:92
  485.7 5.4 copy-start.7
  500.0 5.2 slice-start
  500.0 5.2 slice-start.1
  500.0 7.7 slice-start.2
  520.5 5.4 copy-start.7
  534.9 6.0 slice-start
  534.9 6.0 slice-start.1
  534.9 10.4 slice-start.2
  551.7 4.6 copy-start.1
  551.8 52.8 %all-to-all-start.4 = ((bf16[1024,1,5,128]{3,2,1,0:T(8,128)(2,1)}), bf16[1024,1,5,128]{3,2,1,0:T(8,128)(2,1)}, u32[]{:S(2)}, u32[]{:S(2)}) async-start(bf16[1024,1,5,128]{3,2,1,0:T(8,128)(2,1)} %copy.110), calls=%async_computation.4 | async-start | bytes 4194304 | tf_op jit(solution)/shard_map/all_to_all | solution.py:106
  559.5 49.5 %copy-start.2 = (f32[1024,5,128]{0,2,1:T(8,128)S(1)}, f32[1024,5,128]{0,2,1:T(8,128)}, u32[]{:S(2)}) copy-start(f32[1024,5,128]{0,2,1:T(8,128)} %get-tuple-element.76) | copy-start | bytes 7864324
  604.5 52.2 %all-to-all-start.5 = ((bf16[1024,1,5,128]{3,2,1,0:T(8,128)(2,1)}), bf16[1024,1,5,128]{3,2,1,0:T(8,128)(2,1)}, u32[]{:S(2)}, u32[]{:S(2)}) async-start(bf16[1024,1,5,128]{3,2,1,0:T(8,128)(2,1)} %bitcast.208), calls=%async_computation.5 | async-start | bytes 4194304 | tf_op jit(solution)/shard_map/all_to_all | solution.py:109
  656.8 51.3 %all-to-all-start.6 = ((bf16[1024,1,5,128]{3,2,1,0:T(8,128)(2,1)}), bf16[1024,1,5,128]{3,2,1,0:T(8,128)(2,1)S(1)}, u32[]{:S(2)}, u32[]{:S(2)}) async-start(bf16[1024,1,5,128]{3,2,1,0:T(8,128)(2,1)} %bitcast.207), calls=%async_computation.6 | async-start | bytes 4194304 | tf_op jit(solution)/shard_map/all_to_all | solution.py:116
  (11 other events, 29.1 us)
Sparse Core Ops, SparseCore 0:
  85.4 240.2 all-reduce.4
  328.4 936.0 all-reduce.6
